TPU v7x, 256 devices: a whole 4x4x8 slice. The times are simulated.
256 devices in a mesh: row: 16 (over y, z_lo, core), col: 16 (over x, z_hi).
Axes of the slice: x: 4, y: 4, z: 8 (z_hi: 4, z_lo: 2; z = z_hi * 2 + z_lo), core: 2. Of those that a mesh axis runs over, the one named last changes fastest.
Arguments:
- amplitudes: float32 [8192, 8192], P('row', 'col'), may hold values from -8 to 8, as said below
- factors: float32 [8192, 1536], P(('row', 'col')), may hold values from -1.5 to 1.5
- occ_map: int32 [8192], P(('row', 'col')), may hold values from 0 to 127
- vir_map: int32 [8192], P(('row', 'col')), may hold values from 0 to 1023
- occ_energy: float32 [128], replicated, may hold values from -2 to -0.3
- vir_energy: float32 [1024], replicated, may hold values from 0.2 to 3
Outputs:
- new_amplitudes: float32 [8192, 8192], P('row', 'col')
- density: float32 [8192, 1536], P('row', 'col')
Inputs may be any that keep to these rules, and one draw needn't show every extreme that they name: amplitudes equals its transpose, up to float32 rounding.
All inputs are finite; a program needn't handle non-finite values.
Results may differ from a plain program's by a relative error of at most 0.00012.
Values sent between devices are 32-bit elements; how exact they have to be, the bound alone decides.
No kernel may reach another device: no remote copies, remote signals or barrier semaphores. Data moves between devices by JAX's collectives and lax.ppermute only.
A program may use at most 64 MiB of HBM per device.

v0:
```python
import jax
import jax.numpy as jnp
from jax import lax
from jax.sharding import Mesh, PartitionSpec as P

HIGH = lax.Precision.HIGH
COL = ("x", "deep")
ALL = ("pair", "core", *COL)
CORES = 2
RING = 4


def look_up(table, index):
    hot = index[:, None] == jnp.arange(table.shape[0], dtype=jnp.int32)[None, :]
    return jnp.sum(jnp.where(hot, table[None, :], 0.0), axis=1)


def mul(a, b, da, db):
    return lax.dot_general(
        a, b, (((da,), (db,)), ((), ())), precision=HIGH, preferred_element_type=jnp.float32
    )


def per_device(amplitudes, factors, occ_map, vir_map, occ_energy, vir_energy):
    pairs, n = lax.axis_size("pair"), lax.axis_size(COL)
    core = lax.axis_index("core")
    rows, naux = factors.shape
    half = naux // CORES
    ring = lax.axis_size("x")
    flip_pairs = [(i * n + j, j * n + i) for i in range(n) for j in range(n)]
    swap_pairs = [(0, 1), (1, 0)]
    home_pairs = [
        ((p * CORES + c) * n + j, j * n + c * pairs + p)
        for p in range(pairs)
        for c in range(CORES)
        for j in range(n)
    ]

    def flip(x):
        return lax.ppermute(x, ALL, flip_pairs)

    def swap(x):
        return lax.ppermute(x, "core", swap_pairs)

    def both(own, other, axis):
        first = jnp.where(core == 0, own, other)
        second = jnp.where(core == 0, other, own)
        return jnp.stack([first, second], axis=axis)

    def split_factors(x):
        own = lax.dynamic_slice_in_dim(x, core * half, half, axis=1)
        away = lax.dynamic_slice_in_dim(x, (1 - core) * half, half, axis=1)
        return both(own, swap(away), 0).reshape(CORES * x.shape[0], half)

    def spread(x, axis, copies):
        x = jnp.broadcast_to(x[None], (copies, *x.shape))
        x = x.reshape(copies * x.shape[1], x.shape[2])
        return lax.all_to_all(x, axis, 0, 0, tiled=True)

    def sum_over_pairs(x):
        parts = lax.all_to_all(x, "pair", 0, 0, tiled=True)
        return jnp.sum(parts.reshape(pairs, x.shape[0] // pairs, x.shape[1]), axis=0)

    def shift(x, by):
        return lax.ppermute(x, "x", [(k, (k + by) % ring) for k in range(ring)])

    def ring_gather(x):
        left, right = shift(x, 1), shift(x, -1)
        part = x.shape[0] // 2
        across = [shift(right[:part], -1), shift(left[part:], 1)]
        at = lax.axis_index("x")
        out = jnp.zeros((ring, *x.shape), x.dtype)
        for by, row, block in (
            (0, 0, x), (3, 0, left), (1, 0, right), (2, 0, across[0]), (2, part, across[1])
        ):
            where = (lax.rem(at + by, ring), row, 0)
            out = lax.dynamic_update_slice(out, block[None], where)
        return out.reshape(ring * x.shape[0], x.shape[1]), left, right

    piece, far_amp = lax.optimization_barrier((split_factors(factors), swap(amplitudes)))
    near = lax.all_gather(piece, "deep", axis=0, tiled=True)
    row_factor, left, right = ring_gather(near)
    energy = look_up(vir_energy, vir_map) - look_up(occ_energy, occ_map)
    energy = jnp.broadcast_to(jnp.pad(energy, (0, 128 - rows))[None], (8, 128))
    energy, _ = lax.optimization_barrier((energy, near))
    row_energy = spread(energy, COL, n).reshape(n, 8, 128)[:, 0, :rows].reshape(1, n * rows)

    tile = amplitudes.shape[0]
    width = amplitudes.shape[1]
    own_amp = amplitudes.reshape(n, rows, width)
    far_amp = far_amp.reshape(n, rows, width)
    diagonal = (lax.axis_index(COL) - CORES * lax.axis_index("pair")) == jnp.arange(CORES)
    half_unit = 0.5 * jnp.eye(tile, width, dtype=jnp.float32).reshape(n, 1, rows, width)
    amp = both(own_amp, far_amp, 1) + jnp.where(diagonal[None, :, None, None], half_unit, 0.0)
    amp = amp.reshape(CORES * tile, width)

    amp, row_energy, _, _ = lax.optimization_barrier((amp, row_energy, left, right))

    col_x = spread(sum_over_pairs(mul(amp, row_factor, 0, 0)), "pair", pairs)
    by_core = row_factor.reshape(n, CORES, rows, half)
    own, far = [
        lax.dynamic_index_in_dim(by_core, c, 1, keepdims=False).reshape(tile, half)
        for c in (core, 1 - core)
    ]

    away = swap(mul(col_x, far, 1, 1))
    outgoing = away + lax.optimization_barrier(mul(col_x, own, 1, 1))
    arrived = flip(outgoing)
    local = swap(mul(far, col_x, 1, 1)) + mul(own, col_x, 1, 1)
    row_energy, local = lax.optimization_barrier((row_energy, local))
    col_energy = flip(jnp.broadcast_to(row_energy, (8, width)))[:1]
    new_amp = -(arrived + local) / (row_energy.T + col_energy)
    dens = mul(far, swap(new_amp), 0, 0) + mul(own, new_amp, 0, 0)
    density = lax.ppermute(sum_over_pairs(dens), ALL, home_pairs).T
    return (new_amp, density)


def solution(mesh):
    shape = mesh.devices.shape
    grid = Mesh(mesh.devices.reshape(shape[0] // CORES, CORES, RING, shape[1] // RING), ALL)
    rows = ("pair", "core")
    placed = (
        P(rows, COL),
        P(ALL, None),
        P(ALL),
        P(ALL),
        P(),
        P(),
    )
    return jax.shard_map(
        per_device,
        mesh=grid,
        in_specs=placed,
        out_specs=(P(rows, COL), P(rows, COL)),
        check_vma=False,
    )
```

profile of v0, /device:TPU:38, one launch (start us, length us, event | category | flops | bytes accessed | tf_op | source)
XLA Modules:
  0.0 224.1 jit_solution(5001490459195850378)
XLA Ops:
  6.1 24.3 %all_gather.3 = f32[256,768]{1,0:T(8,128)} all-gather(f32[64,768]{1,0:T(8,128)S(1)} %bitcast.67), channel_id=1, replica_groups=mesh['pair'=8,'core'=2,'x'=4,'deep'=4] {'deep'}, dimensions={0}, use_global_device_ids=true | all-gather | bytes 983040 | tf_op jit(solution)/shard_map/all_gather | solution.py:81
  30.8 1.5 collective-permute-start.3
  33.0 6.9 %all-to-all-start = ((f32[16,8,128]{2,1,0:T(8,128)}), f32[16,8,128]{2,1,0:T(8,128)S(1)}, u32[]{:S(2)}, u32[]{:S(2)}) async-start(f32[16,8,128]{2,1,0:T(8,128)} %broadcast_in_dim.109), calls=%async_computation | async-start | bytes 131072 | tf_op jit(solution)/shard_map/all_to_all | solution.py:58
  43.3 1.6 fusion
  44.9 3.7 %all-to-all-done = f32[16,8,128]{2,1,0:T(8,128)S(1)} async-done(((f32[16,8,128]{2,1,0:T(8,128)}), f32[16,8,128]{2,1,0:T(8,128)S(1)}, u32[]{:S(2)}, u32[]{:S(2)}) %all-to-all-start) | async-done | bytes 65568 | tf_op jit(solution)/shard_map/all_to_all | solution.py:58
  50.4 1.8 slice.18
  52.2 2.7 %collective-permute-start.5 = (f32[128,768]{1,0:T(8,128)}, f32[128,768]{1,0:T(8,128)}, u32[]{:S(2)}, u32[]{:S(2)}) collective-permute-start(f32[128,768]{1,0:T(8,128)} %slice.18), channel_id=1, source_target_pairs={{0,4},{4,8},{8,12},{12,0},{1,5},{5,9},{9,13},{13,1},{2,6},{6,10},{... | collective-permute-start | bytes 1179656 | tf_op jit(solution)/shard_map/ppermute | solution.py:65
  56.0 2.9 %copy.10 = f32[512,1024]{1,0:T(8,128)} copy(f32[512,1024]{0,1:T(8,128)} %bitcast.62) | data formatting | bytes 4194304 | tf_op jit(solution)/shard_map/dot_general | solution.py:19
  62.4 2.8 %fusion.2 = f32[8,64,768]{2,1,0:T(8,128)S(1)} fusion(f32[8,64,1024]{2,1,0:T(8,128)S(1)} %bitcast.63, f32[1024,768,1]{1,0,2:T(8,128)S(1)} %bitcast.54), kind=kOutput, calls=%fused_computation.28 | convolution fusion | flops 2415919104 | bytes 6815744 | tf_op jit(solution)/shard_map/dot_general | solution.py:19
  65.2 22.6 %all_to_all.30 = f32[8,64,768]{2,1,0:T(8,128)} all-to-all(f32[8,64,768]{2,1,0:T(8,128)S(1)} %fusion.2), channel_id=1, replica_groups=mesh['pair'=8,'core'=2,'x'=4,'deep'=4] {'pair'}, dimensions={0} | all-to-all | bytes 3145728 | tf_op jit(solution)/shard_map/all_to_all | solution.py:61
  87.9 1.5 reduce_sum.38
  90.7 4.6 %all-to-all-start.2 = ((f32[8,64,768]{2,1,0:T(8,128)}), f32[8,64,768]{2,1,0:T(8,128)S(1)}, u32[]{:S(2)}, u32[]{:S(2)}) async-start(f32[8,64,768]{2,1,0:T(8,128)} %broadcast_in_dim.116), calls=%async_computation.2 | async-start | bytes 3145728 | tf_op jit(solution)/shard_map/all_to_all | solution.py:58
  95.3 3.3 %constant_dynamic-slice_fusion = (f32[16,1,32,768]{3,2,1,0:T(8,128)}, f32[16,1,32,768]{3,2,1,0:T(8,128)S(1)}) fusion(f32[16,2,32,768]{3,2,1,0:T(8,128)} %bitcast.55, s32[]{:T(128)S(6)} %select_n.101, s32[]{:T(128)S(6)} %select_n.100), kind=kLoop, calls=%fused_computation.24 | loop fusion | bytes 6291464 | tf_op jit(solution)/shard_map/jit(dynamic_index_in_dim)/dynamic_slice | solution.py:102
  98.7 12.3 %all-to-all-done.2 = f32[8,64,768]{2,1,0:T(8,128)S(1)} async-done(((f32[8,64,768]{2,1,0:T(8,128)}), f32[8,64,768]{2,1,0:T(8,128)S(1)}, u32[]{:S(2)}, u32[]{:S(2)}) %all-to-all-start.2) | async-done | bytes 1572896 | tf_op jit(solution)/shard_map/all_to_all | solution.py:58
  114.7 1.5 fusion.4
  116.4 6.9 %collective-permute-start.7 = (f32[512,512]{1,0:T(8,128)S(1)}, f32[512,512]{1,0:T(8,128)S(1)}, u32[]{:S(2)}, u32[]{:S(2)}) collective-permute-start(f32[512,512]{1,0:T(8,128)S(1)} %add.92), channel_id=1, source_target_pairs={{0,0},{1,16},{2,32},{3,48},{4,64},{5,80},{6,96},{7,112},{8,128},{9... | collective-permute-start | bytes 3145736 | tf_op jit(solution)/shard_map/ppermute | solution.py:40
  123.3 1.4 convolution_add_fusion.1
  124.7 6.2 %collective-permute-start.9 = (f32[8,512]{1,0:T(8,128)S(1)}, f32[8,512]{1,0:T(8,128)S(1)}, u32[]{:S(2)}, u32[]{:S(2)}) collective-permute-start(f32[8,512]{1,0:T(8,128)S(1)} %broadcast_in_dim.117), channel_id=1, source_target_pairs={{0,0},{1,16},{2,32},{3,48},{4,64},{5,80},{6,96},{7,112},{8,128},{9... | collective-permute-start | bytes 49160 | tf_op jit(solution)/shard_map/ppermute | solution.py:40
  131.0 40.9 %collective-permute-done.9 = f32[8,512]{1,0:T(8,128)S(1)} collective-permute-done((f32[8,512]{1,0:T(8,128)S(1)}, f32[8,512]{1,0:T(8,128)S(1)}, u32[]{:S(2)}, u32[]{:S(2)}) %collective-permute-start.9) | collective-permute-done | bytes 16416 | tf_op jit(solution)/shard_map/ppermute | solution.py:40
  172.3 1.5 fusion.6
  174.9 1.5 convolution_add_fusion
  176.4 26.6 %all_to_all.31 = f32[8,96,512]{2,1,0:T(8,128)S(1)} all-to-all(f32[8,96,512]{2,1,0:T(8,128)S(1)} %bitcast.64), channel_id=1, replica_groups=mesh['pair'=8,'core'=2,'x'=4,'deep'=4] {'pair'}, dimensions={0} | all-to-all | bytes 3145728 | tf_op jit(solution)/shard_map/all_to_all | solution.py:61
  203.1 2.1 collective-permute-start.11
  205.2 18.2 %collective-permute-done.11 = f32[96,512]{1,0:T(8,128)S(1)} collective-permute-done((f32[96,512]{1,0:T(8,128)S(1)}, f32[96,512]{1,0:T(8,128)S(1)}, u32[]{:S(2)}, u32[]{:S(2)}) %collective-permute-start.11) | collective-permute-done | bytes 196640 | tf_op jit(solution)/shard_map/ppermute | solution.py:114
  (67 shorter events, 23.8 us)
Async XLA Ops:
  1.5 3.6 %collective-permute-start = (f32[32,768]{1,0:T(8,128)S(1)}, f32[32,768]{1,0:T(8,128)S(1)}, u32[]{:S(2)}, u32[]{:S(2)}) collective-permute-start(f32[32,768]{1,0:T(8,128)S(1)} %constant_dynamic-slice_fusion.2), channel_id=1, source_target_pairs={{0,16},{16,0},{1,17},{17,1},{2,18},{18,2},{3,19},{19,3},{4,20},{20... | collective-permute-start | bytes 294920 | tf_op jit(solution)/shard_map/ppermute | solution.py:43
  1.6 4.5 %collective-permute-start.1 = (f32[512,512]{1,0:T(8,128)}, f32[512,512]{1,0:T(8,128)S(1)}, u32[]{:S(2)}, u32[]{:S(2)}) collective-permute-start(f32[512,512]{1,0:T(8,128)} %param.6), channel_id=1, source_target_pairs={{0,16},{16,0},{1,17},{17,1},{2,18},{18,2},{3,19},{19,3},{4,20},{20... | collective-permute-start | bytes 3145736 | tf_op jit(solution)/shard_map/ppermute | solution.py:43
  6.1 27.0 %copy-start.6 = (f32[512,512]{1,0:T(8,128)}, f32[512,512]{1,0:T(8,128)S(1)}, u32[]{:S(2)}) copy-start(f32[512,512]{1,0:T(8,128)S(1)} %collective-permute-done.1) | copy-start | bytes 3145732
  30.4 20.0 %collective-permute-start.2 = (f32[256,768]{1,0:T(8,128)}, f32[256,768]{1,0:T(8,128)}, u32[]{:S(2)}, u32[]{:S(2)}) collective-permute-start(f32[256,768]{1,0:T(8,128)} %all_gather.3), channel_id=1, source_target_pairs={{0,4},{4,8},{8,12},{12,0},{1,5},{5,9},{9,13},{13,1},{2,6},{6,10},{... | collective-permute-start | bytes 2359304 | tf_op jit(solution)/shard_map/ppermute | solution.py:65
  30.8 17.9 %collective-permute-start.3 = (f32[256,768]{1,0:T(8,128)}, f32[256,768]{1,0:T(8,128)}, u32[]{:S(2)}, u32[]{:S(2)}) collective-permute-start(f32[256,768]{1,0:T(8,128)} %all_gather.3), channel_id=1, source_target_pairs={{0,12},{4,0},{8,4},{12,8},{1,13},{5,1},{9,5},{13,9},{2,14},{6,2},{... | collective-permute-start | bytes 2359304 | tf_op jit(solution)/shard_map/ppermute | solution.py:65
  33.0 15.6 %all-to-all-start = ((f32[16,8,128]{2,1,0:T(8,128)}), f32[16,8,128]{2,1,0:T(8,128)S(1)}, u32[]{:S(2)}, u32[]{:S(2)}) async-start(f32[16,8,128]{2,1,0:T(8,128)} %broadcast_in_dim.109), calls=%async_computation | async-start | bytes 131072 | tf_op jit(solution)/shard_map/all_to_all | solution.py:58
  39.9 1.6 copy-start.7
  40.2 1.6 copy-start.5
  42.1 1.2 copy-start.3
  49.7 10.5 %collective-permute-start.4 = (f32[128,768]{1,0:T(8,128)S(1)}, f32[128,768]{1,0:T(8,128)}, u32[]{:S(2)}, u32[]{:S(2)}) collective-permute-start(f32[128,768]{1,0:T(8,128)S(1)} %slice.17), channel_id=1, source_target_pairs={{0,12},{4,0},{8,4},{12,8},{1,13},{5,1},{9,5},{13,9},{2,14},{6,2},{... | collective-permute-start | bytes 1179656 | tf_op jit(solution)/shard_map/ppermute | solution.py:65
  52.2 9.2 %collective-permute-start.5 = (f32[128,768]{1,0:T(8,128)}, f32[128,768]{1,0:T(8,128)}, u32[]{:S(2)}, u32[]{:S(2)}) collective-permute-start(f32[128,768]{1,0:T(8,128)} %slice.18), channel_id=1, source_target_pairs={{0,4},{4,8},{8,12},{12,0},{1,5},{5,9},{9,13},{13,1},{2,6},{6,10},{... | collective-permute-start | bytes 1179656 | tf_op jit(solution)/shard_map/ppermute | solution.py:65
  59.0 3.4 %copy-start.2 = (f32[512,1024]{1,0:T(8,128)S(1)}, f32[512,1024]{1,0:T(8,128)}, u32[]{:S(2)}) copy-start(f32[512,1024]{1,0:T(8,128)} %copy.10) | copy-start | bytes 6291460
  62.4 2.9 %copy-start = (f32[4,256,768]{2,1,0:T(8,128)}, f32[4,256,768]{2,1,0:T(8,128)S(1)}, u32[]{:S(2)}) copy-start(f32[4,256,768]{2,1,0:T(8,128)S(1)} %bitcast_dynamic-update-slice_fusion.3) | copy-start | bytes 9437188
  90.7 20.3 %all-to-all-start.2 = ((f32[8,64,768]{2,1,0:T(8,128)}), f32[8,64,768]{2,1,0:T(8,128)S(1)}, u32[]{:S(2)}, u32[]{:S(2)}) async-start(f32[8,64,768]{2,1,0:T(8,128)} %broadcast_in_dim.116), calls=%async_computation.2 | async-start | bytes 3145728 | tf_op jit(solution)/shard_map/all_to_all | solution.py:58
  112.4 2.3 %copy-start.1 = (f32[16,1,32,768]{3,2,1,0:T(8,128)S(1)}, f32[16,1,32,768]{3,2,1,0:T(8,128)}, u32[]{:S(2)}) copy-start(f32[16,1,32,768]{3,2,1,0:T(8,128)} %get-tuple-element.16) | copy-start | bytes 4718596
  112.4 3.8 %collective-permute-start.6 = (f32[512,512]{1,0:T(8,128)S(1)}, f32[512,512]{1,0:T(8,128)S(1)}, u32[]{:S(2)}, u32[]{:S(2)}) collective-permute-start(f32[512,512]{1,0:T(8,128)S(1)} %fusion.3), channel_id=1, source_target_pairs={{0,16},{16,0},{1,17},{17,1},{2,18},{18,2},{3,19},{19,3},{4,20},{20... | collective-permute-start | bytes 3145736 | tf_op jit(solution)/shard_map/ppermute | solution.py:43
  114.1 9.2 %collective-permute-start.8 = (f32[512,512]{1,0:T(8,128)S(1)}, f32[512,512]{1,0:T(8,128)S(1)}, u32[]{:S(2)}, u32[]{:S(2)}) collective-permute-start(f32[512,512]{1,0:T(8,128)S(1)} %fusion.5), channel_id=1, source_target_pairs={{0,16},{16,0},{1,17},{17,1},{2,18},{18,2},{3,19},{19,3},{4,20},{20... | collective-permute-start | bytes 3145736 | tf_op jit(solution)/shard_map/ppermute | solution.py:43
  116.4 55.4 %collective-permute-start.7 = (f32[512,512]{1,0:T(8,128)S(1)}, f32[512,512]{1,0:T(8,128)S(1)}, u32[]{:S(2)}, u32[]{:S(2)}) collective-permute-start(f32[512,512]{1,0:T(8,128)S(1)} %add.92), channel_id=1, source_target_pairs={{0,0},{1,16},{2,32},{3,48},{4,64},{5,80},{6,96},{7,112},{8,128},{9... | collective-permute-start | bytes 3145736 | tf_op jit(solution)/shard_map/ppermute | solution.py:40
  124.7 47.1 %collective-permute-start.9 = (f32[8,512]{1,0:T(8,128)S(1)}, f32[8,512]{1,0:T(8,128)S(1)}, u32[]{:S(2)}, u32[]{:S(2)}) collective-permute-start(f32[8,512]{1,0:T(8,128)S(1)} %broadcast_in_dim.117), channel_id=1, source_target_pairs={{0,0},{1,16},{2,32},{3,48},{4,64},{5,80},{6,96},{7,112},{8,128},{9... | collective-permute-start | bytes 49160 | tf_op jit(solution)/shard_map/ppermute | solution.py:40
  172.1 1.6 copy-start.4
  172.2 2.7 %collective-permute-start.10 = (f32[512,512]{1,0:T(8,128)S(1)}, f32[512,512]{1,0:T(8,128)S(1)}, u32[]{:S(2)}, u32[]{:S(2)}) collective-permute-start(f32[512,512]{1,0:T(8,128)S(1)} %add_divide_fusion), channel_id=1, source_target_pairs={{0,16},{16,0},{1,17},{17,1},{2,18},{18,2},{3,19},{19,3},{4,20},{20... | collective-permute-start | bytes 3145736 | tf_op jit(solution)/shard_map/ppermute | solution.py:43
  203.1 20.4 %collective-permute-start.11 = (f32[96,512]{1,0:T(8,128)S(1)}, f32[96,512]{1,0:T(8,128)S(1)}, u32[]{:S(2)}, u32[]{:S(2)}) collective-permute-start(f32[96,512]{1,0:T(8,128)S(1)} %reduce_sum.39), channel_id=1, source_target_pairs={{0,0},{1,16},{2,32},{3,48},{4,64},{5,80},{6,96},{7,112},{8,128},{9... | collective-permute-start | bytes 589832 | tf_op jit(solution)/shard_map/ppermute | solution.py:114
where the time goes:
time: 225 us; the launch traced here: 224 us
  waiting for transfers between devices  76.2 us (34%)
  blocking collectives  73.5 us (33%)
  starting transfers between devices  33.6 us (15%)
  local copies, waits for them, and re-layouts  20.2 us (9%)
  matrix products  11.6 us (5%)
  other arithmetic  8.05 us (4%)
    all_to_all x2, blocking collectives, sum_over_pairs(): parts = lax.all_to_all(x, 'pair', 0, 0, tiled=True)  49.2 us
    ppermute x2, waiting for transfers between devices, flip(): return lax.ppermute(x, ALL, flip_pairs)  40.9 us
    all_gather x1, blocking collectives, per_device(): near = lax.all_gather(piece, 'deep', axis=0, tiled=True)  24.3 us
    ppermute x1, waiting for transfers between devices, per_device(): density = lax.ppermute(sum_over_pairs(dens), ALL, home_pairs).T  18.2 us
    all_to_all x2, waiting for transfers between devices, spread(): return lax.all_to_all(x, axis, 0, 0, tiled=True)  16 us
    ppermute x2, starting transfers between devices, flip(): return lax.ppermute(x, ALL, flip_pairs)  13.1 us
    dot_general x7, matrix products, mul(): lax.dot_general(a, b, (((da,), (db,)), ((), ())), precision=HIGH, preferr...  11.6 us
    all_to_all x2, starting transfers between devices, spread(): return lax.all_to_all(x, axis, 0, 0, tiled=True)  11.6 us
  transfers between devices with their start and end apart: 14, of which 5 were waited for; matrix products, arithmetic and copies ran while one was open for 12% of the time, Pallas kernels for 0%

commit v1 on v0

--- a/solution.py
+++ b/solution.py
@@ -89,9 +89,11 @@
     width = amplitudes.shape[1]
     own_amp = amplitudes.reshape(n, rows, width)
     far_amp = far_amp.reshape(n, rows, width)
-    diagonal = (lax.axis_index(COL) - CORES * lax.axis_index("pair")) == jnp.arange(CORES)
-    half_unit = 0.5 * jnp.eye(tile, width, dtype=jnp.float32).reshape(n, 1, rows, width)
-    amp = both(own_amp, far_amp, 1) + jnp.where(diagonal[None, :, None, None], half_unit, 0.0)
+    amp = both(own_amp, far_amp, 1)
+    place = [lax.broadcasted_iota(jnp.int32, amp.shape, k) for k in range(4)]
+    mine = place[1] == lax.axis_index(COL) - CORES * lax.axis_index("pair")
+    diagonal = mine & (place[0] * rows + place[2] == place[3])
+    amp = amp + jnp.where(diagonal, 0.5, 0.0)
     amp = amp.reshape(CORES * tile, width)
 
     amp, row_energy, _, _ = lax.optimization_barrier((amp, row_energy, left, right))

time: 225 us -> 223 us (level)
  transfers between devices with their start and end apart: 14 -> 14, of which waited for: 5 -> 5; matrix products, arithmetic and copies ran while one was open for 12% -> 13% of each run, Pallas kernels for 0% -> 0%
where the time goes in v1:
time: 223 us
  waiting for transfers between devices  76.2 us (34%)
  blocking collectives  72 us (32%)
  starting transfers between devices  34.3 us (15%)
  local copies, waits for them, and re-layouts  19 us (9%)
  matrix products  11.5 us (5%)
  other arithmetic  8.63 us (4%)
    all_to_all x2, blocking collectives, sum_over_pairs(): parts = lax.all_to_all(x, 'pair', 0, 0, tiled=True)  47.7 us
    ppermute x2, waiting for transfers between devices, flip(): return lax.ppermute(x, ALL, flip_pairs)  41.4 us
    all_gather x1, blocking collectives, per_device(): near = lax.all_gather(piece, 'deep', axis=0, tiled=True)  24.3 us
    ppermute x1, waiting for transfers between devices, per_device(): density = lax.ppermute(sum_over_pairs(dens), ALL, home_pairs).T  17.6 us
    all_to_all x2, waiting for transfers between devices, spread(): return lax.all_to_all(x, axis, 0, 0, tiled=True)  15.9 us
    ppermute x2, starting transfers between devices, flip(): return lax.ppermute(x, ALL, flip_pairs)  13.1 us
    all_to_all x2, starting transfers between devices, spread(): return lax.all_to_all(x, axis, 0, 0, tiled=True)  11.6 us
    dot_general x7, matrix products, mul(): lax.dot_general(a, b, (((da,), (db,)), ((), ())), precision=HIGH, preferr...  11.5 us
  transfers between devices with their start and end apart: 14, of which 5 were waited for; matrix products, arithmetic and copies ran while one was open for 13% of the time, Pallas kernels for 0%

profile of v1, /device:TPU:38, one launch (start us, length us, event | category | flops | bytes accessed | tf_op | source)
XLA Modules:
  0.0 222.6 jit_solution(16256518767189644741)
XLA Ops:
  5.2 24.3 %all_gather.3 = f32[256,768]{1,0:T(8,128)} all-gather(f32[64,768]{1,0:T(8,128)S(1)} %bitcast.63), channel_id=1, replica_groups=mesh['pair'=8,'core'=2,'x'=4,'deep'=4] {'deep'}, dimensions={0}, use_global_device_ids=true | all-gather | bytes 983040 | tf_op jit(solution)/shard_map/all_gather | solution.py:81
  30.0 1.5 collective-permute-start.3
  31.5 1.4 broadcast_select_fusion.1
  33.6 6.9 %all-to-all-start = ((f32[16,8,128]{2,1,0:T(8,128)}), f32[16,8,128]{2,1,0:T(8,128)S(1)}, u32[]{:S(2)}, u32[]{:S(2)}) async-start(f32[16,8,128]{2,1,0:T(8,128)} %broadcast_in_dim.86), calls=%async_computation | async-start | bytes 131072 | tf_op jit(solution)/shard_map/all_to_all | solution.py:58
  40.8 2.0 bitcast_add_fusion
  44.2 4.4 %all-to-all-done = f32[16,8,128]{2,1,0:T(8,128)S(1)} async-done(((f32[16,8,128]{2,1,0:T(8,128)}), f32[16,8,128]{2,1,0:T(8,128)S(1)}, u32[]{:S(2)}, u32[]{:S(2)}) %all-to-all-start) | async-done | bytes 65568 | tf_op jit(solution)/shard_map/all_to_all | solution.py:58
  50.5 1.8 slice.18
  52.3 2.5 %collective-permute-start.5 = (f32[128,768]{1,0:T(8,128)}, f32[128,768]{1,0:T(8,128)}, u32[]{:S(2)}, u32[]{:S(2)}) collective-permute-start(f32[128,768]{1,0:T(8,128)} %slice.18), channel_id=1, source_target_pairs={{0,4},{4,8},{8,12},{12,0},{1,5},{5,9},{9,13},{13,1},{2,6},{6,10},{... | collective-permute-start | bytes 1179656 | tf_op jit(solution)/shard_map/ppermute | solution.py:65
  56.0 2.9 %copy.10 = f32[512,1024]{1,0:T(8,128)} copy(f32[512,1024]{0,1:T(8,128)} %bitcast.58) | data formatting | bytes 4194304 | tf_op jit(solution)/shard_map/dot_general | solution.py:19
  62.4 2.8 %fusion.1 = f32[8,64,768]{2,1,0:T(8,128)S(1)} fusion(f32[8,64,1024]{2,1,0:T(8,128)S(1)} %bitcast.59, f32[1024,768,1]{1,0,2:T(8,128)S(1)} %bitcast.50), kind=kOutput, calls=%fused_computation.28 | convolution fusion | flops 2415919104 | bytes 6815744 | tf_op jit(solution)/shard_map/dot_general | solution.py:19
  65.2 21.7 %all_to_all.30 = f32[8,64,768]{2,1,0:T(8,128)} all-to-all(f32[8,64,768]{2,1,0:T(8,128)S(1)} %fusion.1), channel_id=1, replica_groups=mesh['pair'=8,'core'=2,'x'=4,'deep'=4] {'pair'}, dimensions={0} | all-to-all | bytes 3145728 | tf_op jit(solution)/shard_map/all_to_all | solution.py:61
  86.9 1.5 reduce_sum.38
  89.7 4.7 %all-to-all-start.2 = ((f32[8,64,768]{2,1,0:T(8,128)}), f32[8,64,768]{2,1,0:T(8,128)S(1)}, u32[]{:S(2)}, u32[]{:S(2)}) async-start(f32[8,64,768]{2,1,0:T(8,128)} %broadcast_in_dim.93), calls=%async_computation.2 | async-start | bytes 3145728 | tf_op jit(solution)/shard_map/all_to_all | solution.py:58
  94.4 3.4 %constant_dynamic-slice_fusion = (f32[16,1,32,768]{3,2,1,0:T(8,128)}, f32[16,1,32,768]{3,2,1,0:T(8,128)S(1)}) fusion(f32[16,2,32,768]{3,2,1,0:T(8,128)} %bitcast.51, s32[]{:T(128)S(6)} %select_n.101, s32[]{:T(128)S(6)} %select_n.100), kind=kLoop, calls=%fused_computation.23 | loop fusion | bytes 6291464 | tf_op jit(solution)/shard_map/jit(dynamic_index_in_dim)/dynamic_slice | solution.py:104
  97.8 11.6 %all-to-all-done.2 = f32[8,64,768]{2,1,0:T(8,128)S(1)} async-done(((f32[8,64,768]{2,1,0:T(8,128)}), f32[8,64,768]{2,1,0:T(8,128)S(1)}, u32[]{:S(2)}, u32[]{:S(2)}) %all-to-all-start.2) | async-done | bytes 1572896 | tf_op jit(solution)/shard_map/all_to_all | solution.py:58
  113.1 1.5 fusion.3
  114.8 7.2 %collective-permute-start.7 = (f32[512,512]{1,0:T(8,128)S(1)}, f32[512,512]{1,0:T(8,128)S(1)}, u32[]{:S(2)}, u32[]{:S(2)}) collective-permute-start(f32[512,512]{1,0:T(8,128)S(1)} %add.98), channel_id=1, source_target_pairs={{0,0},{1,16},{2,32},{3,48},{4,64},{5,80},{6,96},{7,112},{8,128},{9... | collective-permute-start | bytes 3145736 | tf_op jit(solution)/shard_map/ppermute | solution.py:40
  123.5 5.9 %collective-permute-start.9 = (f32[8,512]{1,0:T(8,128)S(1)}, f32[8,512]{1,0:T(8,128)S(1)}, u32[]{:S(2)}, u32[]{:S(2)}) collective-permute-start(f32[8,512]{1,0:T(8,128)S(1)} %broadcast_in_dim.94), channel_id=1, source_target_pairs={{0,0},{1,16},{2,32},{3,48},{4,64},{5,80},{6,96},{7,112},{8,128},{9... | collective-permute-start | bytes 49160 | tf_op jit(solution)/shard_map/ppermute | solution.py:40
  129.4 41.4 %collective-permute-done.9 = f32[8,512]{1,0:T(8,128)S(1)} collective-permute-done((f32[8,512]{1,0:T(8,128)S(1)}, f32[8,512]{1,0:T(8,128)S(1)}, u32[]{:S(2)}, u32[]{:S(2)}) %collective-permute-start.9) | collective-permute-done | bytes 16416 | tf_op jit(solution)/shard_map/ppermute | solution.py:40
  171.3 1.5 fusion.5
  173.9 1.5 convolution_add_fusion
  175.4 26.0 %all_to_all.31 = f32[8,96,512]{2,1,0:T(8,128)S(1)} all-to-all(f32[8,96,512]{2,1,0:T(8,128)S(1)} %bitcast.60), channel_id=1, replica_groups=mesh['pair'=8,'core'=2,'x'=4,'deep'=4] {'pair'}, dimensions={0} | all-to-all | bytes 3145728 | tf_op jit(solution)/shard_map/all_to_all | solution.py:61
  201.5 2.8 %collective-permute-start.11 = (f32[96,512]{1,0:T(8,128)S(1)}, f32[96,512]{1,0:T(8,128)S(1)}, u32[]{:S(2)}, u32[]{:S(2)}) collective-permute-start(f32[96,512]{1,0:T(8,128)S(1)} %reduce_sum.39), channel_id=1, source_target_pairs={{0,0},{1,16},{2,32},{3,48},{4,64},{5,80},{6,96},{7,112},{8,128},{9... | collective-permute-start | bytes 589832 | tf_op jit(solution)/shard_map/ppermute | solution.py:116
  204.4 17.6 %collective-permute-done.11 = f32[96,512]{1,0:T(8,128)S(1)} collective-permute-done((f32[96,512]{1,0:T(8,128)S(1)}, f32[96,512]{1,0:T(8,128)S(1)}, u32[]{:S(2)}, u32[]{:S(2)}) %collective-permute-start.11) | collective-permute-done | bytes 196640 | tf_op jit(solution)/shard_map/ppermute | solution.py:116
  (64 shorter events, 22.9 us)
Async XLA Ops:
  0.6 30.9 %copy-start.4 = (f32[512,512]{1,0:T(8,128)S(1)}, f32[512,512]{1,0:T(8,128)}, u32[]{:S(2)}) copy-start(f32[512,512]{1,0:T(8,128)} %param.6) | copy-start | bytes 3145732
  0.6 4.6 %collective-permute-start.1 = (f32[512,512]{1,0:T(8,128)}, f32[512,512]{1,0:T(8,128)S(1)}, u32[]{:S(2)}, u32[]{:S(2)}) collective-permute-start(f32[512,512]{1,0:T(8,128)} %param.6), channel_id=1, source_target_pairs={{0,16},{16,0},{1,17},{17,1},{2,18},{18,2},{3,19},{19,3},{4,20},{20... | collective-permute-start | bytes 3145736 | tf_op jit(solution)/shard_map/ppermute | solution.py:43
  1.7 2.5 %collective-permute-start = (f32[32,768]{1,0:T(8,128)S(1)}, f32[32,768]{1,0:T(8,128)S(1)}, u32[]{:S(2)}, u32[]{:S(2)}) collective-permute-start(f32[32,768]{1,0:T(8,128)S(1)} %constant_dynamic-slice_fusion.2), channel_id=1, source_target_pairs={{0,16},{16,0},{1,17},{17,1},{2,18},{18,2},{3,19},{19,3},{4,20},{20... | collective-permute-start | bytes 294920 | tf_op jit(solution)/shard_map/ppermute | solution.py:43
  5.2 24.8 %copy-start.5 = (f32[512,512]{1,0:T(8,128)}, f32[512,512]{1,0:T(8,128)S(1)}, u32[]{:S(2)}) copy-start(f32[512,512]{1,0:T(8,128)S(1)} %collective-permute-done.1) | copy-start | bytes 3145732
  29.5 21.0 %collective-permute-start.2 = (f32[256,768]{1,0:T(8,128)}, f32[256,768]{1,0:T(8,128)}, u32[]{:S(2)}, u32[]{:S(2)}) collective-permute-start(f32[256,768]{1,0:T(8,128)} %all_gather.3), channel_id=1, source_target_pairs={{0,4},{4,8},{8,12},{12,0},{1,5},{5,9},{9,13},{13,1},{2,6},{6,10},{... | collective-permute-start | bytes 2359304 | tf_op jit(solution)/shard_map/ppermute | solution.py:65
  30.0 18.7 %collective-permute-start.3 = (f32[256,768]{1,0:T(8,128)}, f32[256,768]{1,0:T(8,128)}, u32[]{:S(2)}, u32[]{:S(2)}) collective-permute-start(f32[256,768]{1,0:T(8,128)} %all_gather.3), channel_id=1, source_target_pairs={{0,12},{4,0},{8,4},{12,8},{1,13},{5,1},{9,5},{13,9},{2,14},{6,2},{... | collective-permute-start | bytes 2359304 | tf_op jit(solution)/shard_map/ppermute | solution.py:65
  33.6 15.0 %all-to-all-start = ((f32[16,8,128]{2,1,0:T(8,128)}), f32[16,8,128]{2,1,0:T(8,128)S(1)}, u32[]{:S(2)}, u32[]{:S(2)}) async-start(f32[16,8,128]{2,1,0:T(8,128)} %broadcast_in_dim.86), calls=%async_computation | async-start | bytes 131072 | tf_op jit(solution)/shard_map/all_to_all | solution.py:58
  49.7 10.5 %collective-permute-start.4 = (f32[128,768]{1,0:T(8,128)S(1)}, f32[128,768]{1,0:T(8,128)}, u32[]{:S(2)}, u32[]{:S(2)}) collective-permute-start(f32[128,768]{1,0:T(8,128)S(1)} %slice.17), channel_id=1, source_target_pairs={{0,12},{4,0},{8,4},{12,8},{1,13},{5,1},{9,5},{13,9},{2,14},{6,2},{... | collective-permute-start | bytes 1179656 | tf_op jit(solution)/shard_map/ppermute | solution.py:65
  52.3 9.0 %collective-permute-start.5 = (f32[128,768]{1,0:T(8,128)}, f32[128,768]{1,0:T(8,128)}, u32[]{:S(2)}, u32[]{:S(2)}) collective-permute-start(f32[128,768]{1,0:T(8,128)} %slice.18), channel_id=1, source_target_pairs={{0,4},{4,8},{8,12},{12,0},{1,5},{5,9},{9,13},{13,1},{2,6},{6,10},{... | collective-permute-start | bytes 1179656 | tf_op jit(solution)/shard_map/ppermute | solution.py:65
  58.9 3.4 %copy-start.2 = (f32[512,1024]{1,0:T(8,128)S(1)}, f32[512,1024]{1,0:T(8,128)}, u32[]{:S(2)}) copy-start(f32[512,1024]{1,0:T(8,128)} %copy.10) | copy-start | bytes 6291460
  62.3 2.9 %copy-start = (f32[4,256,768]{2,1,0:T(8,128)}, f32[4,256,768]{2,1,0:T(8,128)S(1)}, u32[]{:S(2)}) copy-start(f32[4,256,768]{2,1,0:T(8,128)S(1)} %bitcast_dynamic-update-slice_fusion.3) | copy-start | bytes 9437188
  89.7 19.7 %all-to-all-start.2 = ((f32[8,64,768]{2,1,0:T(8,128)}), f32[8,64,768]{2,1,0:T(8,128)S(1)}, u32[]{:S(2)}, u32[]{:S(2)}) async-start(f32[8,64,768]{2,1,0:T(8,128)} %broadcast_in_dim.93), calls=%async_computation.2 | async-start | bytes 3145728 | tf_op jit(solution)/shard_map/all_to_all | solution.py:58
  110.8 2.3 %copy-start.1 = (f32[16,1,32,768]{3,2,1,0:T(8,128)S(1)}, f32[16,1,32,768]{3,2,1,0:T(8,128)}, u32[]{:S(2)}) copy-start(f32[16,1,32,768]{3,2,1,0:T(8,128)} %get-tuple-element.16) | copy-start | bytes 4718596
  110.8 3.8 %collective-permute-start.6 = (f32[512,512]{1,0:T(8,128)S(1)}, f32[512,512]{1,0:T(8,128)S(1)}, u32[]{:S(2)}, u32[]{:S(2)}) collective-permute-start(f32[512,512]{1,0:T(8,128)S(1)} %fusion.2), channel_id=1, source_target_pairs={{0,16},{16,0},{1,17},{17,1},{2,18},{18,2},{3,19},{19,3},{4,20},{20... | collective-permute-start | bytes 3145736 | tf_op jit(solution)/shard_map/ppermute | solution.py:43
  112.5 9.5 %collective-permute-start.8 = (f32[512,512]{1,0:T(8,128)S(1)}, f32[512,512]{1,0:T(8,128)S(1)}, u32[]{:S(2)}, u32[]{:S(2)}) collective-permute-start(f32[512,512]{1,0:T(8,128)S(1)} %fusion.4), channel_id=1, source_target_pairs={{0,16},{16,0},{1,17},{17,1},{2,18},{18,2},{3,19},{19,3},{4,20},{20... | collective-permute-start | bytes 3145736 | tf_op jit(solution)/shard_map/ppermute | solution.py:43
  114.8 56.0 %collective-permute-start.7 = (f32[512,512]{1,0:T(8,128)S(1)}, f32[512,512]{1,0:T(8,128)S(1)}, u32[]{:S(2)}, u32[]{:S(2)}) collective-permute-start(f32[512,512]{1,0:T(8,128)S(1)} %add.98), channel_id=1, source_target_pairs={{0,0},{1,16},{2,32},{3,48},{4,64},{5,80},{6,96},{7,112},{8,128},{9... | collective-permute-start | bytes 3145736 | tf_op jit(solution)/shard_map/ppermute | solution.py:40
  123.5 47.3 %collective-permute-start.9 = (f32[8,512]{1,0:T(8,128)S(1)}, f32[8,512]{1,0:T(8,128)S(1)}, u32[]{:S(2)}, u32[]{:S(2)}) collective-permute-start(f32[8,512]{1,0:T(8,128)S(1)} %broadcast_in_dim.94), channel_id=1, source_target_pairs={{0,0},{1,16},{2,32},{3,48},{4,64},{5,80},{6,96},{7,112},{8,128},{9... | collective-permute-start | bytes 49160 | tf_op jit(solution)/shard_map/ppermute | solution.py:40
  171.1 1.6 copy-start.3
  171.2 2.7 %collective-permute-start.10 = (f32[512,512]{1,0:T(8,128)S(1)}, f32[512,512]{1,0:T(8,128)S(1)}, u32[]{:S(2)}, u32[]{:S(2)}) collective-permute-start(f32[512,512]{1,0:T(8,128)S(1)} %add_divide_fusion), channel_id=1, source_target_pairs={{0,16},{16,0},{1,17},{17,1},{2,18},{18,2},{3,19},{19,3},{4,20},{20... | collective-permute-start | bytes 3145736 | tf_op jit(solution)/shard_map/ppermute | solution.py:43
  201.5 20.4 %collective-permute-start.11 = (f32[96,512]{1,0:T(8,128)S(1)}, f32[96,512]{1,0:T(8,128)S(1)}, u32[]{:S(2)}, u32[]{:S(2)}) collective-permute-start(f32[96,512]{1,0:T(8,128)S(1)} %reduce_sum.39), channel_id=1, source_target_pairs={{0,0},{1,16},{2,32},{3,48},{4,64},{5,80},{6,96},{7,112},{8,128},{9... | collective-permute-start | bytes 589832 | tf_op jit(solution)/shard_map/ppermute | solution.py:116
